TPU v7x, 256 devices: a whole 4x4x8 slice. The times are simulated.
256 devices in a mesh: band: 8 (over y, x_lo), slab: 32 (over x_hi, z, core).
Axes of the slice: x: 4 (x_hi: 2, x_lo: 2; x = x_hi * 2 + x_lo), y: 4, z: 8, core: 2. Of those that a mesh axis runs over, the one named last changes fastest.
Arguments:
- wavefunctions: float32 [8, 128, 128, 128], P('band', 'slab'), may hold values from -6 to 6
Outputs:
- exchange_field: float32 [8, 128, 128, 128], P('band', 'slab')
All inputs are finite; a program needn't handle non-finite values.
Results may differ from a plain program's by a relative error of at most 0.0003.
Values sent between devices are 32-bit elements; how exact they have to be, the bound alone decides.
A program may use at most 64 MiB of HBM per device.

v0:
```python
import jax
import jax.numpy as jnp
import ml_dtypes
import numpy as np
from jax import lax
from jax.experimental import pallas as pl
from jax.experimental.pallas import tpu as pltpu
from jax.sharding import PartitionSpec as P

MESH = pl.DeviceIdType.MESH
N = 128
CHIPS = 128
BF16, F32 = jnp.bfloat16, jnp.float32

INNER = [((0, 0), (1, 1)), ((2, 2), (3, 3)), ((0, 1), (2, 3)), ((0, 2), (1, 3)), ((0, 3), (1, 2))]
CROSS = 4
COUNTS = (len(INNER), CROSS)
PITCH = tuple(-(-2 * count // 8) * 8 for count in COUNTS)


def weight_tables():
    index = np.arange(N)
    angle = 2.0 * np.pi / N * (index[:, None] * index[None, :] % N)
    cos, sin = np.cos(angle), np.sin(angle)
    forward = np.block([[cos, sin], [-sin, cos]])
    tables = []
    for stage in (forward, forward.T):
        high = stage.astype(ml_dtypes.bfloat16)
        tables += [high, (stage - high.astype(np.float64)).astype(ml_dtypes.bfloat16)]
    return np.stack(tables)


def halves(value):
    high = value.astype(BF16)
    return high, (value - high.astype(F32)).astype(BF16)


def mm(a, b):
    return jnp.dot(a, b, preferred_element_type=F32)


def kernel(own, tables, out, wt, vis, kern, tot, part, take, send_f0, recv_f0, send_f1, recv_f1, send_b0, recv_b0,
           send_b1, recv_b1, table_sem, gather_send, gather_recv, pass_send, pass_recv, trans_send, trans_recv, local_sem,
           swap_send, swap_recv, give_send, give_recv, ready):
    band, slab = lax.axis_index("band"), lax.axis_index("slab")
    core, column = lax.rem(slab, 2), lax.div(slab, 2)
    z, x_hi = lax.rem(column, 8), lax.div(column, 8)
    y, x = lax.div(band, 2), x_hi * 2 + lax.rem(band, 2)
    home, slot = lax.div(band, 4), lax.rem(band, 4)
    me = column * 8 + band
    at = lambda b, s: {"band": b, "slab": s}
    sibling = at(band, column * 2 + 1 - core)

    load = pltpu.make_async_copy(tables, wt, table_sem)
    load.start()

    barrier = pltpu.get_barrier_semaphore()

    def greet_group(k, _):
        j = lax.rem(band * 2 + core + k, 16)
        pl.semaphore_signal(barrier, inc=1, device_id=at(lax.div(j, 2), column * 2 + lax.rem(j, 2)), device_id_type=MESH)
        return 0

    def greet_column(k, _):
        pl.semaphore_signal(barrier, inc=1, device_id=at(band, lax.rem(slab + 2 * k, 32)), device_id_type=MESH)
        return 0

    lax.fori_loop(1, 16, greet_group, 0)
    lax.fori_loop(1, 16, greet_column, 0)
    pl.semaphore_wait(barrier, 30)

    def gather(q):
        return pltpu.make_async_remote_copy(
            own.at[pl.ds(q * N, N)], vis.at[slot], gather_send.at[q], gather_recv.at[slot],
            device_id=at(4 * core + q, column * 2 + home), device_id_type=MESH)

    def keep(q):
        return pltpu.make_async_copy(own.at[pl.ds(q * N, N)], vis.at[slot], gather_recv.at[slot])

    stays = [jnp.logical_and(band == 4 * core + q, home == core) for q in range(4)]
    for q in range(4):
        pl.when(stays[q])(lambda q=q: keep(q).start())
        pl.when(jnp.logical_not(stays[q]))(lambda q=q: gather(q).start())

    def greet_ready(k, _):
        pl.semaphore_signal(ready, inc=1, device_id=at(lax.rem(band + k, 8), slab), device_id_type=MESH)
        return 0

    lax.fori_loop(1, 8, greet_ready, 0)

    fold = lambda v: jnp.where(v < N // 2, v, v - N).astype(F32)
    rows = lambda dim: lax.broadcasted_iota(jnp.int32, (N, N), dim)
    ky = fold(jnp.zeros((N, N), jnp.int32) + me)
    squared = fold(rows(0)) ** 2 + ky * ky + fold(rows(1)) ** 2
    scale = N**1.5 / 4.0 / float(N) ** 3
    kern[...] = jnp.where(squared > 0, scale / jnp.maximum(squared, 1.0), 0.0)
    tot[...] = jnp.zeros(tot.shape, F32)

    def left(stage, value):
        hi, lo = halves(value)
        return mm(wt[2 * stage], hi) + mm(wt[2 * stage], lo) + mm(wt[2 * stage + 1], hi)

    def right(value, stage):
        hi, lo = halves(value)
        return mm(hi, wt[2 * stage]) + mm(lo, wt[2 * stage]) + mm(hi, wt[2 * stage + 1])

    def wide(values):
        return jnp.concatenate(values, axis=1)

    def tall(values):
        return jnp.concatenate(values, axis=0)

    def put(ref, chunk, field):
        flat = ref.reshape(CHIPS * PITCH[chunk], N)
        for p in range(COUNTS[chunk]):
            for i in range(2):
                flat[pl.ds(2 * p + i, CHIPS, stride=PITCH[chunk]), :] = field[i * N:(i + 1) * N, p * N:(p + 1) * N]

    def get(ref, chunk):
        flat = ref.reshape(CHIPS * PITCH[chunk], N)
        return wide([tall([flat[pl.ds(2 * p + i, CHIPS, stride=PITCH[chunk]), :] for i in range(2)])
                     for p in range(COUNTS[chunk])])

    def analyse(pairs):
        spec = right(tall([wide([a, b]) for a, b in pairs]), 1)
        return left(0, wide([tall([spec[p * N:(p + 1) * N, :N], spec[p * N:(p + 1) * N, N:]]) for p in range(len(pairs))]))

    def convolve(columns):
        spec = left(0, columns)
        table = wide([kern[...]] * (columns.shape[1] // N))
        return left(1, tall([spec[:N] * table, spec[N:] * table]))

    def synthesise(columns):
        spec = left(1, columns)
        count = columns.shape[1] // N
        both = right(tall([wide([spec[:N, p * N:(p + 1) * N], spec[N:, p * N:(p + 1) * N]]) for p in range(count)]), 0)
        return [(both[p * N:(p + 1) * N, :N], both[p * N:(p + 1) * N, N:]) for p in range(count)]

    depths = [lax.rem(z + step, 8) for step in range(8)]

    def exchange(source, target, chunk, sem):
        used = pl.ds(0, 2 * COUNTS[chunk])

        def send(to_x, to_y, step):
            to_band, to_column = to_y * 2 + lax.rem(to_x, 2), lax.div(to_x, 2) * 8 + depths[step]
            pltpu.make_async_remote_copy(
                source.at[to_column * 8 + to_band, used], target.at[me, used], trans_send.at[sem], trans_recv.at[sem],
                device_id=at(to_band, to_column * 2 + core), device_id_type=MESH).start()

        def row(k, _):
            for step in (4, 3, 5, 2, 6, 1, 7, 0):
                send(lax.rem(x + lax.rem(k, 4), 4), lax.rem(y + lax.div(k, 4), 4), step)
            return 0

        lax.fori_loop(1, 16, row, 0)
        for step in (4, 3, 5, 2, 6, 1, 7):
            send(x, y, step)
        pltpu.make_async_copy(source.at[me, used], target.at[me, used], local_sem.at[sem]).start()

    def others(ref, chunk):
        return ref.at[pl.ds(0, CHIPS - 1), pl.ds(0, 2 * COUNTS[chunk])]

    def exchanged(source, target, chunk, sem):
        used = pl.ds(0, 2 * COUNTS[chunk])
        pltpu.make_async_copy(source.at[me, used], target.at[me, used], local_sem.at[sem]).wait()
        pltpu.make_async_copy(others(target, chunk), others(target, chunk), trans_recv.at[sem]).wait()

    def sent(source, chunk, sem):
        pltpu.make_async_copy(others(source, chunk), others(source, chunk), trans_send.at[sem]).wait()

    def hand_on(u):
        return pltpu.make_async_remote_copy(vis.at[u], vis.at[4 + u], pass_send.at[u], pass_recv.at[u],
                                            device_id=sibling, device_id_type=MESH)

    for u in range(4):
        pltpu.make_async_copy(vis.at[u], vis.at[u], gather_recv.at[u]).wait()
        hand_on(u).start()
    load.wait()
    put(send_f0, 0, analyse([tuple(vis[i] * vis[j] for i, j in pair) for pair in INNER]))
    pl.semaphore_wait(ready, 7)
    exchange(send_f0, recv_f0, 0, 0)

    for u in range(4):
        hand_on(u).wait_recv()
    across = [(u, 4 + lax.rem(core + u, 2)) for u in range(4)]
    put(send_f1, 1, analyse([(vis[u] * vis[v], vis[u] * vis[v + 2]) for u, v in across]))
    exchange(send_f1, recv_f1, 1, 1)

    exchanged(send_f0, recv_f0, 0, 0)
    put(send_b0, 0, convolve(get(recv_f0, 0)))
    exchange(send_b0, recv_b0, 0, 2)
    exchanged(send_f1, recv_f1, 1, 1)
    put(send_b1, 1, convolve(get(recv_f1, 1)))
    exchange(send_b1, recv_b1, 1, 3)

    exchanged(send_b0, recv_b0, 0, 2)
    for pair, fields in zip(INNER, synthesise(get(recv_b0, 0))):
        for (i, j), field in zip(pair, fields):
            tot[i] += field * vis[j]
            if i != j:
                tot[j] += field * vis[i]
    exchanged(send_b1, recv_b1, 1, 3)
    for (u, v), (first, second) in zip(across, synthesise(get(recv_b1, 1))):
        tot[u] += first * vis[v] + second * vis[v + 2]
        tot[v] += first * vis[u]
        tot[v + 2] += second * vis[u]

    def swap(u):
        return pltpu.make_async_remote_copy(tot.at[4 + u], part.at[u], swap_send.at[u], swap_recv.at[u],
                                            device_id=sibling, device_id_type=MESH)

    def give(u):
        return pltpu.make_async_remote_copy(
            part.at[u], take.at[pl.ds(slot * N, N)], give_send.at[u], give_recv.at[slot],
            device_id=at(4 * core + u, column * 2 + home), device_id_type=MESH)

    def keep_own(u):
        return pltpu.make_async_copy(part.at[u], take.at[pl.ds(slot * N, N)], give_recv.at[slot])

    for u in range(4):
        swap(u).start()
    for u in range(4):
        swap(u).wait_recv()
        part[u] = -0.25 * (part[u] + tot[u])
        pl.when(stays[u])(lambda u=u: keep_own(u).start())
        pl.when(jnp.logical_not(stays[u]))(lambda u=u: give(u).start())
    for q in range(4):
        block = take.at[pl.ds(q * N, N)]
        pltpu.make_async_copy(block, block, give_recv.at[q]).wait()
    out[...] = take[...]

    for q in range(4):
        pl.when(jnp.logical_not(stays[q]))(lambda q=q: gather(q).wait_send())
        pl.when(jnp.logical_not(stays[q]))(lambda q=q: give(q).wait_send())
        hand_on(q).wait_send()
        swap(q).wait_send()
    sent(send_f0, 0, 0)
    sent(send_f1, 1, 1)
    sent(send_b0, 0, 2)
    sent(send_b1, 1, 3)


def per_device(wavefunctions, tables):
    vmem, anywhere = pl.BlockSpec(memory_space=pltpu.VMEM), pl.BlockSpec(memory_space=pl.ANY)
    dma = pltpu.SemaphoreType.DMA
    chunks = [pltpu.VMEM((CHIPS, pitch, N), F32) for pitch in PITCH]
    planes = lambda count: pltpu.VMEM((count, N, N), F32)
    field = pl.pallas_call(
        kernel,
        out_shape=jax.ShapeDtypeStruct((4 * N, N), F32),
        in_specs=[anywhere, anywhere],
        out_specs=vmem,
        scratch_shapes=[
            pltpu.VMEM(tables.shape, BF16),
            planes(8), pltpu.VMEM((N, N), F32), planes(8), planes(4), pltpu.VMEM((4 * N, N), F32),
            chunks[0], chunks[0], chunks[1], chunks[1], chunks[0], chunks[0], chunks[1], chunks[1],
            dma, dma((4,)), dma((4,)), dma((4,)), dma((4,)), dma((4,)), dma((4,)), dma((4,)),
            dma((4,)), dma((4,)), dma((4,)), dma((4,)), pltpu.SemaphoreType.REGULAR,
        ],
        compiler_params=pltpu.CompilerParams(collective_id=0, has_side_effects=True, vmem_limit_bytes=48 << 20),
        name="exchange",
    )(wavefunctions.reshape(4 * N, N), tables)
    return field.reshape(1, 4, N, N)


def solution(mesh):
    tables = weight_tables()
    spec = P("band", "slab", None, None)
    run = jax.shard_map(per_device, mesh=mesh, in_specs=(spec, P()), out_specs=spec, check_vma=False)
    return lambda wavefunctions: run(wavefunctions, jnp.asarray(tables))
```

profile of v0, /device:TPU:1, one launch (start us, length us, event | category | flops | bytes accessed | tf_op | source)
XLA Modules:
  0.0 81.6 jit_solution(15136553068627501873)
XLA Ops:
  0.0 0.0 copy-start
  0.0 1.0 %copy-done = bf16[4,256,256]{2,1,0:T(8,128)(2,1)S(1)} copy-done((bf16[4,256,256]{2,1,0:T(8,128)(2,1)S(1)}, bf16[4,256,256]{2,1,0:T(8,128)(2,1)}, u32[]{:S(2)}) %copy-start) | copy-done | bytes 524312
  1.0 0.0 copy-start.1
  1.0 0.9 %copy-done.1 = f32[1,4,128,128]{3,2,1,0:T(8,128)S(1)} copy-done((f32[1,4,128,128]{3,2,1,0:T(8,128)S(1)}, f32[1,4,128,128]{3,2,1,0:T(8,128)}, u32[]{:S(2)}) %copy-start.1) | copy-done | bytes 262168
  2.0 78.9 %exchange.1 = f32[512,128]{1,0:T(8,128)S(1)} custom-call(f32[512,128]{1,0:T(8,128)S(1)} %bitcast.3, bf16[4,256,256]{2,1,0:T(8,128)(2,1)S(1)} %copy-done), custom_call_target="tpu_custom_call" | custom-call | tf_op jit(solution)/shard_map/exchange/pallas_call | solution.py:248
  80.9 0.7 copy.4
Async XLA Ops:
  0.0 1.0 %copy-start = (bf16[4,256,256]{2,1,0:T(8,128)(2,1)S(1)}, bf16[4,256,256]{2,1,0:T(8,128)(2,1)}, u32[]{:S(2)}) copy-start(bf16[4,256,256]{2,1,0:T(8,128)(2,1)} %constant.2.clone.tables) | copy-start | bytes 1572868
  1.0 0.9 %copy-start.1 = (f32[1,4,128,128]{3,2,1,0:T(8,128)S(1)}, f32[1,4,128,128]{3,2,1,0:T(8,128)}, u32[]{:S(2)}) copy-start(f32[1,4,128,128]{3,2,1,0:T(8,128)} %param.2) | copy-start | bytes 786436
where the time goes:
time: 81.7 us; the launch traced here: 81.6 us
  Pallas kernels  78.9 us (97%)
  local copies, waits for them, and re-layouts  2.7 us (3%)
    pallas_call x1, Pallas kernels, per_device(): pl.pallas_call(kernel, out_shape=jax.ShapeDtypeStruct((4 * N, N), F32), i...  78.9 us
    unnamed x5, local copies, waits for them, and re-layouts  2.7 us

commit v1 on v0

--- a/solution.py
+++ b/solution.py
@@ -12,10 +12,10 @@
 CHIPS = 128
 BF16, F32 = jnp.bfloat16, jnp.float32
 
-INNER = [((0, 0), (1, 1)), ((2, 2), (3, 3)), ((0, 1), (2, 3)), ((0, 2), (1, 3)), ((0, 3), (1, 2))]
-CROSS = 4
-COUNTS = (len(INNER), CROSS)
-PITCH = tuple(-(-2 * count // 8) * 8 for count in COUNTS)
+INNER = [((0, 0), (1, 1)), ((0, 1), (2, 3)), ((0, 2), (1, 3)), ((0, 3), (1, 2))]
+LAST = [((2, 2), (3, 3))]
+COUNTS = (len(INNER), 4, len(LAST))
+PITCH = tuple(8 if count > 1 else 2 for count in COUNTS)
 
 
 def weight_tables():
@@ -39,8 +39,8 @@
     return jnp.dot(a, b, preferred_element_type=F32)
 
 
-def kernel(own, tables, out, wt, vis, kern, tot, part, take, send_f0, recv_f0, send_f1, recv_f1, send_b0, recv_b0,
-           send_b1, recv_b1, table_sem, gather_send, gather_recv, pass_send, pass_recv, trans_send, trans_recv, local_sem,
+def kernel(own, tables, out, wt, vis, kern, tot, part, take, send_f0, recv_f0, send_f1, recv_f1, send_f2, recv_f2,
+           send_b0, recv_b0, send_b1, recv_b1, send_b2, recv_b2, table_sem, gather_send, gather_recv, pass_send, pass_recv, trans_send, trans_recv, local_sem,
            swap_send, swap_recv, give_send, give_recv, ready):
     band, slab = lax.axis_index("band"), lax.axis_index("slab")
     core, column = lax.rem(slab, 2), lax.div(slab, 2)
@@ -69,18 +69,21 @@
     lax.fori_loop(1, 16, greet_column, 0)
     pl.semaphore_wait(barrier, 30)
 
-    def gather(q):
+    turned = [lax.rem(slot + i, 4) for i in range(4)]
+    stays = home == core
+
+    def gather(i):
         return pltpu.make_async_remote_copy(
-            own.at[pl.ds(q * N, N)], vis.at[slot], gather_send.at[q], gather_recv.at[slot],
-            device_id=at(4 * core + q, column * 2 + home), device_id_type=MESH)
-
-    def keep(q):
-        return pltpu.make_async_copy(own.at[pl.ds(q * N, N)], vis.at[slot], gather_recv.at[slot])
-
-    stays = [jnp.logical_and(band == 4 * core + q, home == core) for q in range(4)]
-    for q in range(4):
-        pl.when(stays[q])(lambda q=q: keep(q).start())
-        pl.when(jnp.logical_not(stays[q]))(lambda q=q: gather(q).start())
+            own.at[pl.ds(turned[i] * N, N)], vis.at[slot], gather_send.at[i], gather_recv.at[slot],
+            device_id=at(4 * core + turned[i], column * 2 + home), device_id_type=MESH)
+
+    def unless_stays(remote, local):
+        pl.when(stays)(lambda: local.start())
+        pl.when(jnp.logical_not(stays))(lambda: remote.start())
+
+    for i in range(1, 4):
+        gather(i).start()
+    unless_stays(gather(0), pltpu.make_async_copy(own.at[pl.ds(slot * N, N)], vis.at[slot], gather_recv.at[slot]))
 
     def greet_ready(k, _):
         pl.semaphore_signal(ready, inc=1, device_id=at(lax.rem(band + k, 8), slab), device_id_type=MESH)
@@ -185,21 +188,29 @@
     across = [(u, 4 + lax.rem(core + u, 2)) for u in range(4)]
     put(send_f1, 1, analyse([(vis[u] * vis[v], vis[u] * vis[v + 2]) for u, v in across]))
     exchange(send_f1, recv_f1, 1, 1)
+    put(send_f2, 2, analyse([tuple(vis[i] * vis[j] for i, j in pair) for pair in LAST]))
+    exchange(send_f2, recv_f2, 2, 2)
 
     exchanged(send_f0, recv_f0, 0, 0)
     put(send_b0, 0, convolve(get(recv_f0, 0)))
-    exchange(send_b0, recv_b0, 0, 2)
+    exchange(send_b0, recv_b0, 0, 3)
     exchanged(send_f1, recv_f1, 1, 1)
     put(send_b1, 1, convolve(get(recv_f1, 1)))
-    exchange(send_b1, recv_b1, 1, 3)
-
-    exchanged(send_b0, recv_b0, 0, 2)
-    for pair, fields in zip(INNER, synthesise(get(recv_b0, 0))):
-        for (i, j), field in zip(pair, fields):
-            tot[i] += field * vis[j]
-            if i != j:
-                tot[j] += field * vis[i]
-    exchanged(send_b1, recv_b1, 1, 3)
+    exchange(send_b1, recv_b1, 1, 4)
+    exchanged(send_f2, recv_f2, 2, 2)
+    put(send_b2, 2, convolve(get(recv_f2, 2)))
+    exchange(send_b2, recv_b2, 2, 5)
+
+    def collect(pairs, columns):
+        for pair, fields in zip(pairs, synthesise(columns)):
+            for (i, j), field in zip(pair, fields):
+                tot[i] += field * vis[j]
+                if i != j:
+                    tot[j] += field * vis[i]
+
+    exchanged(send_b0, recv_b0, 0, 3)
+    collect(INNER, get(recv_b0, 0))
+    exchanged(send_b1, recv_b1, 1, 4)
     for (u, v), (first, second) in zip(across, synthesise(get(recv_b1, 1))):
         tot[u] += first * vis[v] + second * vis[v + 2]
         tot[v] += first * vis[u]
@@ -209,57 +220,71 @@
         return pltpu.make_async_remote_copy(tot.at[4 + u], part.at[u], swap_send.at[u], swap_recv.at[u],
                                             device_id=sibling, device_id_type=MESH)
 
+    mine = take.at[pl.ds(slot * N, N)]
+
     def give(u):
         return pltpu.make_async_remote_copy(
-            part.at[u], take.at[pl.ds(slot * N, N)], give_send.at[u], give_recv.at[slot],
+            part.at[u], mine, give_send.at[u], give_recv.at[slot],
             device_id=at(4 * core + u, column * 2 + home), device_id_type=MESH)
 
-    def keep_own(u):
-        return pltpu.make_async_copy(part.at[u], take.at[pl.ds(slot * N, N)], give_recv.at[slot])
+    def finish(u):
+        part[u] = -0.25 * (part[u] + tot[u])
+        here = jnp.logical_and(stays, slot == u)
+        pl.when(here)(lambda: pltpu.make_async_copy(part.at[u], mine, give_recv.at[slot]).start())
+        pl.when(jnp.logical_not(here))(lambda: give(u).start())
 
     for u in range(4):
         swap(u).start()
     for u in range(4):
         swap(u).wait_recv()
-        part[u] = -0.25 * (part[u] + tot[u])
-        pl.when(stays[u])(lambda u=u: keep_own(u).start())
-        pl.when(jnp.logical_not(stays[u]))(lambda u=u: give(u).start())
+    flip = lax.rem(slot, 2)
+    finish(flip)
+    finish(1 - flip)
+    exchanged(send_b2, recv_b2, 2, 5)
+    collect(LAST, get(recv_b2, 2))
+    finish(2 + flip)
+    finish(3 - flip)
     for q in range(4):
         block = take.at[pl.ds(q * N, N)]
         pltpu.make_async_copy(block, block, give_recv.at[q]).wait()
     out[...] = take[...]
 
     for q in range(4):
-        pl.when(jnp.logical_not(stays[q]))(lambda q=q: gather(q).wait_send())
-        pl.when(jnp.logical_not(stays[q]))(lambda q=q: give(q).wait_send())
+        if q == 0:
+            pl.when(jnp.logical_not(stays))(lambda: gather(0).wait_send())
+        else:
+            gather(q).wait_send()
+        pl.when(jnp.logical_not(jnp.logical_and(stays, slot == q)))(lambda q=q: give(q).wait_send())
         hand_on(q).wait_send()
         swap(q).wait_send()
     sent(send_f0, 0, 0)
     sent(send_f1, 1, 1)
-    sent(send_b0, 0, 2)
-    sent(send_b1, 1, 3)
+    sent(send_f2, 2, 2)
+    sent(send_b0, 0, 3)
+    sent(send_b1, 1, 4)
+    sent(send_b2, 2, 5)
 
 
 def per_device(wavefunctions, tables):
-    vmem, anywhere = pl.BlockSpec(memory_space=pltpu.VMEM), pl.BlockSpec(memory_space=pl.ANY)
+    vmem, far = pl.BlockSpec(memory_space=pltpu.VMEM), pl.BlockSpec(memory_space=pltpu.HBM)
     dma = pltpu.SemaphoreType.DMA
     chunks = [pltpu.VMEM((CHIPS, pitch, N), F32) for pitch in PITCH]
     planes = lambda count: pltpu.VMEM((count, N, N), F32)
     field = pl.pallas_call(
         kernel,
         out_shape=jax.ShapeDtypeStruct((4 * N, N), F32),
-        in_specs=[anywhere, anywhere],
+        in_specs=[far, far],
         out_specs=vmem,
         scratch_shapes=[
             pltpu.VMEM(tables.shape, BF16),
             planes(8), pltpu.VMEM((N, N), F32), planes(8), planes(4), pltpu.VMEM((4 * N, N), F32),
-            chunks[0], chunks[0], chunks[1], chunks[1], chunks[0], chunks[0], chunks[1], chunks[1],
-            dma, dma((4,)), dma((4,)), dma((4,)), dma((4,)), dma((4,)), dma((4,)), dma((4,)),
+            *[chunk for chunk in chunks * 2 for _ in range(2)],
+            dma, dma((4,)), dma((4,)), dma((4,)), dma((4,)), dma((6,)), dma((6,)), dma((6,)),
             dma((4,)), dma((4,)), dma((4,)), dma((4,)), pltpu.SemaphoreType.REGULAR,
         ],
         compiler_params=pltpu.CompilerParams(collective_id=0, has_side_effects=True, vmem_limit_bytes=48 << 20),
         name="exchange",
-    )(wavefunctions.reshape(4 * N, N), tables)
+    )(*[pltpu.with_memory_space_constraint(value, pltpu.HBM) for value in (wavefunctions.reshape(4 * N, N), tables)])
     return field.reshape(1, 4, N, N)
 
 

time: 81.7 us -> 77.6 us (0.950)
  Pallas kernels: 78.9 us -> 76.8 us
  local copies, waits for them, and re-layouts: 2.7 us -> 0.71 us
    pallas_call x1, Pallas kernels: 78.9 us -> 76.8 us  [per_device(): pl.pallas_call(kernel, out_shape=jax.ShapeDtypeStruct((4 * N, N), F32), i...]
    unnamed x5 -> x1, local copies, waits for them, and re-layouts: 2.7 us -> 0.71 us
where the time goes in v1:
time: 77.6 us; the launch traced here: 77.5 us
  Pallas kernels  76.8 us (99%)
    pallas_call x1, Pallas kernels, per_device(): pl.pallas_call(kernel, out_shape=jax.ShapeDtypeStruct((4 * N, N), F32), i...  76.8 us

profile of v1, /device:TPU:1, one launch (start us, length us, event | category | flops | bytes accessed | tf_op | source)
XLA Modules:
  0.0 77.5 jit_solution(17512584757161057897)
XLA Ops:
  0.0 76.8 %exchange.1 = f32[512,128]{1,0:T(8,128)S(1)} custom-call(f32[512,128]{1,0:T(8,128)} %bitcast.3, bf16[4,256,256]{2,1,0:T(8,128)(2,1)} %constant.2.clone.tables), custom_call_target="tpu_custom_call" | custom-call | tf_op jit(solution)/shard_map/exchange/pallas_call | solution.py:273
  76.8 0.7 copy.4
